TPU v7x, 1024 devices: a whole 4x8x16 slice. The times are simulated.
1024 devices in a mesh: dp: 64 (over x, z_lo, core), tensor: 16 (over y, z_hi).
Axes of the slice: x: 4, y: 8, z: 16 (z_hi: 2, z_lo: 8; z = z_hi * 8 + z_lo), core: 2. Of those that a mesh axis runs over, the one named last changes fastest.
Arguments:
- inputs: bfloat16 [1280, 6144], P('dp', 'tensor'), may hold values from -6 to 6
- cotangent: bfloat16 [1280, 6144], P('dp', 'tensor'), may hold values from -6 to 6
- up_weight: bfloat16 [6144, 24576], P('tensor', 'dp'), may hold values from -0.078125 to 0.078125
- down_weight: bfloat16 [24576, 6144], P('dp', 'tensor'), may hold values from -0.078125 to 0.078125
- up_bias: float32 [24576], P('dp'), may hold values from -4 to 4
Outputs:
- input_grad: bfloat16 [1280, 6144], P('dp', 'tensor')
All inputs are finite; a program needn't handle non-finite values.
Results may differ from a plain program's by a relative error of at most 0.024.
Values may be sent and summed in bfloat16 or wider, within the bound.
A program may use at most 32 MiB of HBM per device.

v0:
```python
import jax
import jax.numpy as jnp
from jax import lax
from jax.sharding import PartitionSpec as P


def gelu_tanh(v):
    return jax.nn.gelu(v, approximate=True)


def hidden_from(totals, up_bias):
    pre_act = totals[0] + up_bias[None, :]
    _, back = jax.vjp(gelu_tanh, pre_act)
    return back(totals[1])[0].astype(jnp.bfloat16)


def body(inputs, cotangent, up_weight, down_weight, up_bias):
    stacked = jnp.stack([inputs, cotangent])
    piece = lax.all_gather(stacked, "dp", axis=1, tiled=True)
    part_pre = jnp.dot(piece[0], up_weight, preferred_element_type=jnp.float32)
    part_up = lax.dot_general(
        piece[1], down_weight, (((1,), (1,)), ((), ())), preferred_element_type=jnp.float32
    )
    partials = jnp.stack([part_pre, part_up])
    shares = lax.psum_scatter(
        partials.astype(jnp.bfloat16), "tensor", scatter_dimension=1, tiled=True
    ).astype(jnp.float32)
    hidden_grad = lax.all_gather(hidden_from(shares, up_bias), "tensor", axis=0, tiled=True)
    summed = lax.psum_scatter(
        lax.dot_general(
            hidden_grad, up_weight, (((1,), (1,)), ((), ())), preferred_element_type=jnp.float32
        ),
        "dp",
        scatter_dimension=0,
        tiled=True,
    )
    return summed.astype(jnp.bfloat16)


def solution(mesh):
    return jax.shard_map(
        body,
        mesh=mesh,
        in_specs=(
            P("dp", "tensor"),
            P("dp", "tensor"),
            P("tensor", "dp"),
            P("dp", "tensor"),
            P("dp"),
        ),
        out_specs=P("dp", "tensor"),
        check_vma=False,
    )
```

profile of v0, /device:TPU:1, one launch (start us, length us, event | category | flops | bytes accessed | tf_op | source)
XLA Modules:
  0.0 977.8 jit_solution(229377374356904062)
XLA Ops:
  6.5 0.0 copy-start
  6.5 0.0 all-gather.2.cloned.1.call-start
  6.5 0.8 pad_maximum_fusion.1
  7.3 0.6 copy.6
  8.0 0.0 all-gather.2.cloned.1.call-update
  8.0 0.0 reduce-scatter.2.cloned.1.call-start
  8.0 135.3 %all-gather.2.cloned.1.call-done = bf16[2,1280,384]{2,0,1:T(2,128)(2,1)} async-done(((bf16[2,20,384]{2,0,1:T(2,128)(2,1)}), bf16[2,1280,384]{2,0,1:T(2,128)(2,1)}) %all-gather.2.cloned.1.call-update) | async-done | bytes 1966096 | tf_op jit(solution)/shard_map/all_gather | solution.py:19
  143.4 5.3 fusion.10
  148.7 0.0 copy-start.1
  148.7 0.0 copy-done
  148.7 0.7 fusion
  149.4 0.2 copy-done.1
  149.6 0.8 fusion.1
  150.4 1.5 pad_maximum_fusion
  151.9 0.0 copy-start.2
  151.9 0.0 reduce-scatter.2.cloned.1.call-update
  151.9 1.3 dynamic-slice
  153.9 244.6 %reduce-scatter.2.cloned.1.call-done = bf16[2,80,384]{2,1,0:T(8,128)(2,1)} async-done(((bf16[2,1280,384]{2,1,0:T(8,128)(2,1)}), bf16[2,80,384]{2,1,0:T(8,128)(2,1)}) %reduce-scatter.2.cloned.1.call-update) | async-done | bytes 122896 | tf_op jit(solution)/shard_map/reduce_scatter | solution.py:25
  398.5 0.9 convert_element_type.10
  399.4 0.0 copy-done.2
  399.4 0.1 fusion.8
  399.5 125.8 %all_gather.7 = bf16[1280,384]{1,0:T(8,128)(2,1)S(1)} all-gather(bf16[80,384]{1,0:T(8,128)(2,1)S(1)} %fusion.8), channel_id=1, replica_groups=mesh['dp'=64,'tensor'=16] {'tensor'}, dimensions={0}, use_global_device_ids=true | all-gather | bytes 1044480 | tf_op jit(solution)/shard_map/all_gather | solution.py:28
  525.3 0.8 fusion.11
  526.1 444.2 %all-reduce.2 = bf16[1280,384]{1,0:T(8,128)(2,1)S(1)} all-reduce(f32[1280,384]{1,0:T(8,128)S(1)} %fusion.11), channel_id=3, replica_groups=mesh['dp'=64,'tensor'=16] {'dp'}, use_global_device_ids=true, to_apply=%region_1.0.clone | all-reduce | flops 491520 | bytes 2949120
  970.3 0.6 dynamic-slice_convert_fusion
Async XLA Ops:
  6.5 142.1 %copy-start = (bf16[384,384]{1,0:T(8,128)(2,1)S(1)}, bf16[384,384]{1,0:T(8,128)(2,1)}, u32[]{:S(2)}) copy-start(bf16[384,384]{1,0:T(8,128)(2,1)} %param.7) | copy-start | bytes 884740
  6.5 136.9 %all-gather.2.cloned.1.call-start = ((), (), s32[]{:S(2)}) async-start(), calls=%async_computation.1 | async-start | bytes 1996800 | tf_op jit(solution)/shard_map/all_gather | solution.py:19
  8.0 390.5 %reduce-scatter.2.cloned.1.call-start = ((), (), s32[]{:S(2)}) async-start(), calls=%async_computation.2 | async-start | bytes 2088960 | tf_op jit(solution)/shard_map/reduce_scatter | solution.py:25
  148.7 1.0 copy-start.1
  151.9 247.5 %copy-start.2 = (f32[384]{0:T(512)S(1)}, f32[384]{0:T(512)}, u32[]{:S(2)}) copy-start(f32[384]{0:T(512)} %param.9) | copy-start | bytes 4612
Sparse Core Ops, SparseCore 0:
  10.1 133.2 all-gather.1
  152.1 246.3 reduce-scatter.1
where the time goes:
time: 987 us; the launch traced here: 978 us
  blocking collectives  570 us (58%)
  waiting for transfers between devices  380 us (39%)
  between operations  14.1 us (1%)
    unnamed x1, blocking collectives  444 us
    reduce_scatter x1, waiting for transfers between devices, body(): lax.psum_scatter(partials.astype(jnp.bfloat16), 'tensor', scatter_dimensi...  245 us
    all_gather x1, waiting for transfers between devices, body(): piece = lax.all_gather(stacked, 'dp', axis=1, tiled=True)  135 us
    all_gather x1, blocking collectives, body(): lax.all_gather(hidden_from(shares, up_bias), 'tensor', axis=0, tiled=True)  126 us
  transfers between devices with their start and end apart: 2, of which 2 were waited for; matrix products, arithmetic and copies ran while one was open for 0% of the time, Pallas kernels for 0%

commit v1 on v0

v1 whole, which is shorter than its diff:
```python
import functools

import jax
import jax.numpy as jnp
import numpy as np
from jax import lax
from jax.experimental import pallas as pl
from jax.experimental.pallas import tpu as pltpu
from jax.sharding import PartitionSpec as P

MESH = pl.DeviceIdType.MESH
BF16, F32 = jnp.bfloat16, jnp.float32

NX, NZ, NC, NY = 4, 8, 2, 8
OWN = 20
SLAB = 48
W = 384
CHUNKS, SLOTS = 2, 4
BLOCK = SLOTS * OWN
OUT = 32

OFFSETS = ((0, 1, 7, 2), (6, 3, 5, 4))
WHERE = {off: (k, j) for k, row in enumerate(OFFSETS) for j, off in enumerate(row)}

SQRT_2_OVER_PI = 0.7978845608028654
CUBE = 0.044715


def select_matrices():
    pack = np.zeros((2 * BLOCK, SLOTS * SLAB), np.float32)
    spread = np.zeros((SLOTS * OUT, BLOCK), np.float32)
    for j in range(SLOTS):
        for r in range(OWN):
            pack[j * OWN + r, j * SLAB + r] = 1.0
            pack[BLOCK + j * OWN + r, j * SLAB + OWN + r] = 1.0
            spread[j * OUT + r, j * OWN + r] = 1.0
    return jnp.asarray(pack, BF16), jnp.asarray(spread, BF16)


def dot(a, b):
    return jnp.dot(a, b, preferred_element_type=F32)


def dot_t(a, b):
    return lax.dot_general(a, b, (((1,), (1,)), ((), ())), preferred_element_type=F32)


def gelu_slope(v):
    u = SQRT_2_OVER_PI * (v + CUBE * (v * v * v))
    t = jnp.tanh(u)
    du = SQRT_2_OVER_PI * (1.0 + (3.0 * CUBE) * (v * v))
    return 0.5 * (1.0 + t) + 0.5 * v * (1.0 - t * t) * du


def kernel(
    slab_ref, up_ref, down_ref, bias_ref, pack_ref, spread_ref, out_ref,
    gath, part, ysend, yrecv, zsend, zrecv, hid, prod, csend, crecv, xsend, xrecv, fsend, frecv,
    az_s, az_r, ax_s, ax_r, ac_s, ac_r, y_s, y_r, zh_s, zh_r, h_s, h_r, c_s, c_r, x_s, x_r, f_s, f_r,
):
    d, t = lax.axis_index("dp"), lax.axis_index("tensor")
    x, z, c = d // (NZ * NC), (d // NC) % NZ, d % NC
    y, zh = t // 2, t % 2
    ring = jnp.where(z % 2 == 0, z // 2, NZ - 1 - z // 2)

    def dev(x=x, z=z, c=c, y=y, zh=zh):
        return ((x * NZ + z) * NC + c, y * 2 + zh)

    def at_ring(off):
        r = (ring + off) % NZ
        return dev(z=jnp.where(r < NZ // 2, 2 * r, 2 * NZ - 1 - 2 * r))

    def at_x(off):
        return dev(x=(x + off) % NX)

    def at_y(off):
        return dev(y=(y + off) % NY)

    sibling, far = dev(c=1 - c), dev(zh=1 - zh)

    sends = []

    def send(src, dst, ssem, rsem, device):
        copy = pltpu.make_async_remote_copy(
            src_ref=src, dst_ref=dst, send_sem=ssem, recv_sem=rsem, device_id=device, device_id_type=MESH
        )
        copy.start()
        sends.append(copy)

    def arrived(ref, rsem):
        pltpu.make_async_copy(ref, ref, rsem).wait()

    peers = [sibling, far, at_y(1), at_y(-1)]
    peers += [at_x(o) for o in range(1, NX)] + [at_ring(o) for o in range(1, NZ)]
    barrier = pltpu.get_barrier_semaphore()
    for peer in peers:
        pl.semaphore_signal(barrier, inc=1, device_id=peer, device_id_type=MESH)
    gath[0, 0, pl.ds(c, 1), 0:SLAB, :] = slab_ref[...][None]
    pl.semaphore_wait(barrier, len(peers))

    def zslot(off):
        k, j = WHERE[off % NZ]
        return gath.at[k, 0, c, pl.ds(SLAB * j, SLAB)]

    def z_send(off, way):
        src = slab_ref if off == 0 else zslot(off)
        at = (off - way) % NZ
        send(src, zslot(at), az_s.at[at], az_r.at[at], at_ring(way))

    def z_wait(off):
        off %= NZ
        arrived(zslot(off), az_r.at[off])

    HALF = SLOTS * SLAB // 2

    def x_send_own(k):
        for i, way in enumerate((1, -1)):
            send(gath.at[k, 0, c], gath.at[k, -way % NX, c], ax_s.at[k, i], ax_r.at[k, i], at_x(way))

    def x_pass(k, i):
        way = (1, -1)[i]
        q = -way % NX
        arrived(gath.at[k, q, c], ax_r.at[k, i])
        rows = pl.ds(HALF * i, HALF)
        send(gath.at[k, q, c, rows], gath.at[k, 2, c, rows], ax_s.at[k, 2 + i], ax_r.at[k, 2 + i], at_x(way))
        core_send(k, q)

    def x_last(k):
        for i in range(2):
            arrived(gath.at[k, 2, c, pl.ds(HALF * i, HALF)], ax_r.at[k, 2 + i])
        core_send(k, 2)

    def core_send(k, q):
        send(gath.at[k, q, c], gath.at[k, q, c], ac_s.at[k, q], ac_r.at[k, q], sibling)

    def core_wait(k):
        for q in range(NX):
            arrived(gath.at[k, q, 1 - c], ac_r.at[k, q])

    def partial(k, dist):
        o = (y + dist) % NY
        rows = dot(pack_ref[...], gath[k, o // NC, o % NC]).astype(BF16)
        part[k, dist % NY, 0] = dot(rows[:BLOCK], up_ref[...])
        part[k, dist % NY, 1] = dot_t(rows[BLOCK:], down_ref[...])

    def y_step(k, m):
        dist = 4 - (m + 1) // 2
        for i, way in enumerate((1, -1)):
            which = (m + 1 + i) % 2
            total = part[k, (way * dist) % NY, which]
            if m >= 2:
                arrived(yrecv.at[k, i, m - 2], y_r.at[k, i, m - 2])
                total = total + yrecv[k, i, m - 2].astype(F32)
            ysend[k, i, m] = total.astype(BF16)
            send(ysend.at[k, i, m], yrecv.at[k, i, m], y_s.at[k, i, m], y_r.at[k, i, m], at_y(way))

    def y_last(k):
        for i in range(2):
            arrived(yrecv.at[k, i, 5], y_r.at[k, i, 5])
            which = i
            part[k, 0, which] = part[k, 0, which] + yrecv[k, i, 5].astype(F32)
        for i in range(2):
            arrived(yrecv.at[k, i, 6], y_r.at[k, i, 6])
            which = 1 - i
            total = part[k, 0, which] + yrecv[k, i, 6].astype(F32)
            part[k, 0, which] = total
        for which in range(2):
            zsend[k, which] = part[k, 0, which].astype(BF16)
            send(zsend.at[k, which], zrecv.at[k, which], zh_s.at[k, which], zh_r.at[k, which], far)

    def hidden(k):
        arrived(zrecv.at[k, 0], zh_r.at[k, 0])
        slope = gelu_slope(part[k, 0, 0] + zrecv[k, 0].astype(F32) + bias_ref[...])
        arrived(zrecv.at[k, 1], zh_r.at[k, 1])
        value = ((part[k, 0, 1] + zrecv[k, 1].astype(F32)) * slope).astype(BF16)
        hid[k, pl.ds(y, 1)] = value[None]

    def h_piece(k, o, s, i):
        if s < 4:
            return hid.at[k, o % NY]
        return hid.at[k, o % NY, pl.ds(0, 48) if i == 0 else pl.ds(48, 32)]

    def h_send(k, s):
        for i, way in enumerate((1, -1)):
            piece = h_piece(k, y - way * (s - 1) + NY, s, i)
            send(piece, piece, h_s.at[k, i, s - 1], h_r.at[k, i, s - 1], at_y(way))

    def h_wait(k, s):
        for i, way in enumerate((1, -1)):
            arrived(h_piece(k, y - way * s + NY, s, i), h_r.at[k, i, s - 1])

    def product(k):
        @pl.loop(0, NX)
        def _(q):
            for cc in range(NC):
                prod[k, q, cc] = dot_t(hid[k, q * NC + cc], up_ref[...])

        csend[k] = prod[k, :, 1 - c].astype(BF16)
        send(csend.at[k], crecv.at[k], c_s.at[k], c_r.at[k], sibling)

    def over_cores(k):
        arrived(crecv.at[k], c_r.at[k])
        for q in (2, 1, 3, 0):
            total = prod[k, q, c] + crecv[k, q].astype(F32)
            if q == 0:
                prod[k, 0, 0] = total
            else:
                xsend[k, q - 1] = total.astype(BF16)
                send(xsend.at[k, q - 1], xrecv.at[k, q - 1], x_s.at[k, q - 1], x_r.at[k, q - 1], at_x(q))

    def over_x(k):
        total = prod[k, 0, 0]
        for q in (1, 3, 2):
            arrived(xrecv.at[k, q - 1], x_r.at[k, q - 1])
            total = total + xrecv[k, q - 1].astype(F32)
        slabs = dot(spread_ref[...], total.astype(BF16)).astype(BF16)
        fsend[k] = slabs.reshape(SLOTS, OUT, W)
        for j in range(SLOTS):
            off = OFFSETS[k][j]
            if off:
                send(fsend.at[k, j], frecv.at[k, j], f_s.at[k, j], f_r.at[k, j], at_ring(off))

    def over_z():
        total = fsend[0, 0].astype(F32)
        for k in range(CHUNKS):
            for j in range(SLOTS):
                if OFFSETS[k][j]:
                    arrived(frecv.at[k, j], f_r.at[k, j])
                    total = total + frecv[k, j].astype(F32)
        out_ref[...] = total[:OWN].astype(BF16)

    z_send(0, 1)
    z_send(0, -1)
    z_wait(-1)
    z_send(-1, 1)
    z_wait(1)
    z_send(1, -1)
    z_wait(2)
    x_send_own(0)
    z_send(2, -1)
    core_send(0, 0)
    z_wait(-2)
    z_send(-2, 1)
    x_pass(0, 0)
    x_pass(0, 1)
    z_wait(-3)
    z_send(-3, 1)
    z_wait(3)
    x_last(0)
    core_wait(0)
    partial(0, 4)
    y_step(0, 0)
    partial(0, 3)
    partial(0, -3)
    y_step(0, 1)
    z_wait(4)
    x_send_own(1)
    core_send(1, 0)
    y_step(0, 2)
    partial(0, 2)
    partial(0, -2)
    y_step(0, 3)
    y_step(0, 4)
    x_pass(1, 0)
    x_pass(1, 1)
    partial(0, 1)
    partial(0, -1)
    y_step(0, 5)
    y_step(0, 6)
    partial(0, 0)
    x_last(1)
    core_wait(1)
    partial(1, 4)
    y_step(1, 0)
    partial(1, 3)
    partial(1, -3)
    y_step(1, 1)
    y_last(0)
    y_step(1, 2)
    partial(1, 2)
    partial(1, -2)
    y_step(1, 3)
    y_step(1, 4)
    partial(1, 1)
    partial(1, -1)
    partial(1, 0)
    y_step(1, 5)
    y_step(1, 6)
    y_last(1)
    hidden(0)
    for s in range(1, 5):
        h_send(0, s)
        h_wait(0, s)
    product(0)
    hidden(1)
    h_send(1, 1)
    over_cores(0)
    h_wait(1, 1)
    h_send(1, 2)
    over_x(0)
    h_wait(1, 2)
    h_send(1, 3)
    h_wait(1, 3)
    h_send(1, 4)
    h_wait(1, 4)
    product(1)
    over_cores(1)
    over_x(1)
    over_z()
    for copy in sends:
        copy.wait_send()


def body(inputs, cotangent, up_weight, down_weight, up_bias):
    slab = jnp.concatenate([inputs, cotangent, jnp.zeros((SLAB - 2 * OWN, W), BF16)])
    pack, spread = select_matrices()
    vmem, dma = pltpu.VMEM, pltpu.SemaphoreType.DMA
    scratch = [
        vmem((CHUNKS, NX, NC, SLOTS * SLAB, W), BF16),
        vmem((CHUNKS, NY, 2, BLOCK, W), F32),
        vmem((CHUNKS, 2, 7, BLOCK, W), BF16),
        vmem((CHUNKS, 2, 7, BLOCK, W), BF16),
        vmem((CHUNKS, 2, BLOCK, W), BF16),
        vmem((CHUNKS, 2, BLOCK, W), BF16),
        vmem((CHUNKS, NY, BLOCK, W), BF16),
        vmem((CHUNKS, NX, NC, BLOCK, W), F32),
        vmem((CHUNKS, NX, BLOCK, W), BF16),
        vmem((CHUNKS, NX, BLOCK, W), BF16),
        vmem((CHUNKS, NX - 1, BLOCK, W), BF16),
        vmem((CHUNKS, NX - 1, BLOCK, W), BF16),
        vmem((CHUNKS, SLOTS, OUT, W), BF16),
        vmem((CHUNKS, SLOTS, OUT, W), BF16),
    ]
    for shape in (
        (NZ,), (CHUNKS, 4), (CHUNKS, NX), (CHUNKS, 2, 7), (CHUNKS, 2), (CHUNKS, 2, 4),
        (CHUNKS,), (CHUNKS, NX - 1), (CHUNKS, SLOTS),
    ):
        scratch += [dma(shape), dma(shape)]
    return pl.pallas_call(
        kernel,
        out_shape=jax.ShapeDtypeStruct((OWN, W), BF16),
        in_specs=[pl.BlockSpec(memory_space=pltpu.VMEM)] * 6,
        out_specs=pl.BlockSpec(memory_space=pltpu.VMEM),
        scratch_shapes=scratch,
        compiler_params=pltpu.CompilerParams(
            collective_id=0, has_side_effects=True, vmem_limit_bytes=48 << 20
        ),
        name="mlp_input_grad",
    )(slab, up_weight, down_weight, up_bias[None, :], pack, spread)


def solution(mesh):
    return jax.shard_map(
        body,
        mesh=mesh,
        in_specs=(
            P("dp", "tensor"),
            P("dp", "tensor"),
            P("tensor", "dp"),
            P("dp", "tensor"),
            P("dp"),
        ),
        out_specs=P("dp", "tensor"),
        check_vma=False,
    )
```

time: 987 us -> 126 us (0.13)
  blocking collectives: 570 us -> 0 us
  waiting for transfers between devices: 380 us -> 0 us
  Pallas kernels: 0 us -> 121 us
  between operations: 14.1 us -> 0.03 us
    unnamed x1 -> x0, blocking collectives: 444 us -> none
    reduce_scatter x1 -> x0, waiting for transfers between devices: 245 us -> none  [body(): lax.psum_scatter(partials.astype(jnp.bfloat16), 'tensor', scatter_dimensi...]
    all_gather x1 -> x0, waiting for transfers between devices: 135 us -> none  [body(): piece = lax.all_gather(stacked, 'dp', axis=1, tiled=True)]
    all_gather x1 -> x0, blocking collectives: 126 us -> none  [body(): lax.all_gather(hidden_from(shares, up_bias), 'tensor', axis=0, tiled=True)]
    pallas_call x0 -> x1, Pallas kernels: none -> 121 us  [body(): pl.pallas_call(kernel, out_shape=jax.ShapeDtypeStruct((OWN, W), BF16), in...]
  transfers between devices with their start and end apart: 2 -> 0, of which waited for: 2 -> 0; matrix products, arithmetic and copies ran while one was open for 0% -> 0% of each run, Pallas kernels for 0% -> 0%
where the time goes in v1:
time: 126 us
  Pallas kernels  121 us (96%)
  local copies, waits for them, and re-layouts  4.1 us (3%)
    pallas_call x1, Pallas kernels, body(): pl.pallas_call(kernel, out_shape=jax.ShapeDtypeStruct((OWN, W), BF16), in...  121 us
    unnamed x11, local copies, waits for them, and re-layouts  4.02 us

profile of v1, /device:TPU:1, one launch (start us, length us, event | category | flops | bytes accessed | tf_op | source)
XLA Modules:
  0.0 125.8 jit_solution(6247330601075968999)
XLA Ops:
  0.0 0.0 copy-start.4
  0.0 0.1 pad.2.clone
  0.1 0.6 copy-done.4
  0.7 0.0 copy-start.3
  0.7 0.8 maximum_maximum_fusion.slab_ref
  1.5 0.0 copy-done.3
  1.5 0.0 copy-start
  1.5 1.0 copy-done
  2.5 0.0 copy-start.1
  2.5 1.0 copy-done.1
  3.4 0.0 copy-start.2
  3.4 0.9 copy-done.2
  4.3 120.9 %mlp_input_grad.1 = bf16[20,384]{1,0:T(8,128)(2,1)S(1)} custom-call(bf16[48,384]{1,0:T(8,128)(2,1)S(1)} %maximum_maximum_fusion.slab_ref, bf16[384,384]{1,0:T(8,128)(2,1)S(1)} %copy-done, bf16[384,384]{1,0:T(8,128)(2,1)S(1)} %copy-done.1, f32[1,384]{1,0:T(1,128)S(1)} %broadcast_in_dim.7.bias_ref, bf16[160,192]{1,0:T(8,128)(2,1)S(1)} %copy-done.2, ...), custom_call_target="tpu_custom_call" | custom-call | tf_op jit(solution)/shard_map/mlp_input_grad/pallas_call | solution.py:338
  125.2 0.6 copy.9
  (2 shorter events, 0.0 us)
Async XLA Ops:
  0.0 0.7 copy-start.4
  0.7 0.8 copy-start.3
  1.5 1.0 copy-start
  2.5 1.0 copy-start.1
  3.4 0.9 copy-start.2

commit v2 on v1

--- a/solution.py
+++ b/solution.py
@@ -53,9 +53,10 @@
 
 
 def kernel(
-    slab_ref, up_ref, down_ref, bias_ref, pack_ref, spread_ref, out_ref,
+    slab_ref, up_hbm, down_hbm, bias_hbm, pack_hbm, spread_hbm, out_ref,
+    up_ref, down_ref, bias_ref, pack_ref, spread_ref,
     gath, part, ysend, yrecv, zsend, zrecv, hid, prod, csend, crecv, xsend, xrecv, fsend, frecv,
-    az_s, az_r, ax_s, ax_r, ac_s, ac_r, y_s, y_r, zh_s, zh_r, h_s, h_r, c_s, c_r, x_s, x_r, f_s, f_r,
+    az_s, az_r, ax_s, ax_r, ac_s, ac_r, y_s, y_r, zh_s, zh_r, h_s, h_r, c_s, c_r, x_s, x_r, f_s, f_r, load_s,
 ):
     d, t = lax.axis_index("dp"), lax.axis_index("tensor")
     x, z, c = d // (NZ * NC), (d // NC) % NZ, d % NC
@@ -88,6 +89,18 @@
 
     def arrived(ref, rsem):
         pltpu.make_async_copy(ref, ref, rsem).wait()
+
+    def left(src, dst, ssem, rsem, device):
+        pltpu.make_async_remote_copy(
+            src_ref=src, dst_ref=dst, send_sem=ssem, recv_sem=rsem, device_id=device, device_id_type=MESH
+        ).wait_send()
+
+    loads = []
+    for i, (src, dst) in enumerate(
+        ((up_hbm, up_ref), (down_hbm, down_ref), (bias_hbm, bias_ref), (pack_hbm, pack_ref), (spread_hbm, spread_ref))
+    ):
+        loads.append(pltpu.make_async_copy(src, dst, load_s.at[i]))
+        loads[-1].start()
 
     peers = [sibling, far, at_y(1), at_y(-1)]
     peers += [at_x(o) for o in range(1, NX)] + [at_ring(o) for o in range(1, NZ)]
@@ -97,36 +110,49 @@
     gath[0, 0, pl.ds(c, 1), 0:SLAB, :] = slab_ref[...][None]
     pl.semaphore_wait(barrier, len(peers))
 
-    def zslot(off):
+    def slot(off, q=0, rows=SLAB, start=0):
         k, j = WHERE[off % NZ]
-        return gath.at[k, 0, c, pl.ds(SLAB * j, SLAB)]
-
-    def z_send(off, way):
-        src = slab_ref if off == 0 else zslot(off)
-        at = (off - way) % NZ
-        send(src, zslot(at), az_s.at[at], az_r.at[at], at_ring(way))
-
-    def z_wait(off):
+        return gath.at[k, q % NX, c, pl.ds(SLAB * j + start, rows)]
+
+    def z_own():
+        for way in (2, -2, 1, -1):
+            at = -way % NZ
+            send(slab_ref, slot(at), az_s.at[at], az_r.at[at], at_ring(way))
+        x_send(0)
+
+    def z_pass(way):
+        off = -2 * way % NZ
+        arrived(slot(off), az_r.at[off])
+        at = -3 * way % NZ
+        send(slot(off), slot(at), az_s.at[at], az_r.at[at], at_ring(way))
+        rows, start, i = (32, 0, 4) if way == 1 else (16, 32, 0)
+        send(slot(off, 0, rows, start), slot(4, 0, rows, start), az_s.at[i], az_r.at[i], at_ring(2 * way))
+        x_send(off)
+
+    def z_take(off):
         off %= NZ
-        arrived(zslot(off), az_r.at[off])
-
-    HALF = SLOTS * SLAB // 2
-
-    def x_send_own(k):
-        for i, way in enumerate((1, -1)):
-            send(gath.at[k, 0, c], gath.at[k, -way % NX, c], ax_s.at[k, i], ax_r.at[k, i], at_x(way))
-
-    def x_pass(k, i):
-        way = (1, -1)[i]
-        q = -way % NX
-        arrived(gath.at[k, q, c], ax_r.at[k, i])
-        rows = pl.ds(HALF * i, HALF)
-        send(gath.at[k, q, c, rows], gath.at[k, 2, c, rows], ax_s.at[k, 2 + i], ax_r.at[k, 2 + i], at_x(way))
-        core_send(k, q)
+        if off == 4:
+            arrived(slot(4, 0, 32, 0), az_r.at[4])
+            arrived(slot(4, 0, 16, 32), az_r.at[0])
+        else:
+            arrived(slot(off), az_r.at[off])
+        x_send(off)
+
+    def x_send(off):
+        for i, way in enumerate((1, -1)):
+            src = slab_ref if off == 0 else slot(off)
+            send(src, slot(off, -way), ax_s.at[i, off], ax_r.at[i, off], at_x(way))
+
+    def x_take(off):
+        off %= NZ
+        for i, way in enumerate((1, -1)):
+            arrived(slot(off, -way), ax_r.at[i, off])
+            if i == WHERE[off][1] % 2:
+                send(slot(off, -way), slot(off, 2), ax_s.at[2, off], ax_r.at[2, off], at_x(way))
 
     def x_last(k):
-        for i in range(2):
-            arrived(gath.at[k, 2, c, pl.ds(HALF * i, HALF)], ax_r.at[k, 2 + i])
+        for off in OFFSETS[k]:
+            arrived(slot(off, 2), ax_r.at[2, off])
         core_send(k, 2)
 
     def core_send(k, q):
@@ -174,44 +200,65 @@
         value = ((part[k, 0, 1] + zrecv[k, 1].astype(F32)) * slope).astype(BF16)
         hid[k, pl.ds(y, 1)] = value[None]
 
-    def h_piece(k, o, s, i):
-        if s < 4:
-            return hid.at[k, o % NY]
-        return hid.at[k, o % NY, pl.ds(0, 48) if i == 0 else pl.ds(48, 32)]
-
-    def h_send(k, s):
-        for i, way in enumerate((1, -1)):
-            piece = h_piece(k, y - way * (s - 1) + NY, s, i)
-            send(piece, piece, h_s.at[k, i, s - 1], h_r.at[k, i, s - 1], at_y(way))
-
-    def h_wait(k, s):
-        for i, way in enumerate((1, -1)):
-            arrived(h_piece(k, y - way * s + NY, s, i), h_r.at[k, i, s - 1])
-
-    def product(k):
-        @pl.loop(0, NX)
-        def _(q):
-            for cc in range(NC):
-                prod[k, q, cc] = dot_t(hid[k, q * NC + cc], up_ref[...])
-
-        csend[k] = prod[k, :, 1 - c].astype(BF16)
-        send(csend.at[k], crecv.at[k], c_s.at[k], c_r.at[k], sibling)
-
-    def over_cores(k):
-        arrived(crecv.at[k], c_r.at[k])
-        for q in (2, 1, 3, 0):
-            total = prod[k, q, c] + crecv[k, q].astype(F32)
-            if q == 0:
-                prod[k, 0, 0] = total
-            else:
-                xsend[k, q - 1] = total.astype(BF16)
-                send(xsend.at[k, q - 1], xrecv.at[k, q - 1], x_s.at[k, q - 1], x_r.at[k, q - 1], at_x(q))
+    def h_block(k, dist, rows=BLOCK, start=0):
+        return hid.at[k, (y + dist + NY) % NY, pl.ds(start, rows)]
+
+    def h_copy(k, dist, way, i, rows=BLOCK, start=0):
+        piece = h_block(k, dist, rows, start)
+        send(piece, piece, h_s.at[k, i], h_r.at[k, i], at_y(way))
+
+    def h_own(k):
+        for i, way in enumerate((2, -2, 1, -1)):
+            h_copy(k, 0, way, i)
+
+    def h_pass(k):
+        for i, way in enumerate((1, -1)):
+            arrived(h_block(k, -2 * way), h_r.at[k, i])
+            h_copy(k, -2 * way, way, 4 + i)
+            h_copy(k, -2 * way, 2 * way, 6 + i, *((48, 0) if way == 1 else (32, 48)))
+        for i, way in enumerate((1, -1)):
+            arrived(h_block(k, -way), h_r.at[k, 2 + i])
+
+    def h_last(k):
+        for i, way in enumerate((1, -1)):
+            arrived(h_block(k, -3 * way), h_r.at[k, 4 + i])
+            arrived(h_block(k, 4, *((48, 0) if way == 1 else (32, 48))), h_r.at[k, 6 + i])
+
+    def pair(dist, own):
+        first = y + dist + NY
+        o = (first + (first + c + (0 if own else 1)) % 2) % NY
+        return o // NC, o
+
+    def product(k, dist):
+        q, o = pair(dist, False)
+        csend[k, q] = dot_t(hid[k, o], up_ref[...]).astype(BF16)
+        copy = pltpu.make_async_remote_copy(
+            src_ref=csend.at[k, q], dst_ref=crecv.at[k, q], send_sem=c_s.at[k, q], recv_sem=c_r.at[k, q],
+            device_id=sibling, device_id_type=MESH,
+        )
+        copy.start()
+        q, o = pair(dist, True)
+        prod[k, q] = dot_t(hid[k, o], up_ref[...])
+
+    def over_cores(k, dist):
+        q, _ = pair(dist, True)
+        arrived(crecv.at[k, q], c_r.at[k, q])
+        total = prod[k, q] + crecv[k, q].astype(F32)
+        prod[k, q] = total
+        xsend[k, q] = total.astype(BF16)
+
+        @pl.when(q != 0)
+        def _():
+            pltpu.make_async_remote_copy(
+                src_ref=xsend.at[k, q], dst_ref=xrecv.at[k, q], send_sem=x_s.at[k, q], recv_sem=x_r.at[k, q],
+                device_id=at_x(q), device_id_type=MESH,
+            ).start()
 
     def over_x(k):
-        total = prod[k, 0, 0]
+        total = prod[k, 0]
         for q in (1, 3, 2):
-            arrived(xrecv.at[k, q - 1], x_r.at[k, q - 1])
-            total = total + xrecv[k, q - 1].astype(F32)
+            arrived(xrecv.at[k, q], x_r.at[k, q])
+            total = total + xrecv[k, q].astype(F32)
         slabs = dot(spread_ref[...], total.astype(BF16)).astype(BF16)
         fsend[k] = slabs.reshape(SLOTS, OUT, W)
         for j in range(SLOTS):
@@ -228,86 +275,100 @@
                     total = total + frecv[k, j].astype(F32)
         out_ref[...] = total[:OWN].astype(BF16)
 
-    z_send(0, 1)
-    z_send(0, -1)
-    z_wait(-1)
-    z_send(-1, 1)
-    z_wait(1)
-    z_send(1, -1)
-    z_wait(2)
-    x_send_own(0)
-    z_send(2, -1)
+    z_own()
+    x_take(0)
+    z_pass(1)
+    z_pass(-1)
+    z_take(1)
+    z_take(-1)
     core_send(0, 0)
-    z_wait(-2)
-    z_send(-2, 1)
-    x_pass(0, 0)
-    x_pass(0, 1)
-    z_wait(-3)
-    z_send(-3, 1)
-    z_wait(3)
+    x_take(2)
+    x_take(-2)
+    x_take(1)
+    x_take(-1)
+    core_send(0, 1)
+    core_send(0, 3)
+    z_take(3)
+    z_take(-3)
+    z_take(4)
+    core_send(1, 0)
     x_last(0)
+    for load in loads:
+        load.wait()
     core_wait(0)
     partial(0, 4)
     y_step(0, 0)
     partial(0, 3)
     partial(0, -3)
     y_step(0, 1)
-    z_wait(4)
-    x_send_own(1)
-    core_send(1, 0)
-    y_step(0, 2)
+    x_take(3)
+    x_take(-3)
+    x_take(4)
+    core_send(1, 1)
+    core_send(1, 3)
     partial(0, 2)
     partial(0, -2)
+    y_step(0, 2)
     y_step(0, 3)
-    y_step(0, 4)
-    x_pass(1, 0)
-    x_pass(1, 1)
+    x_last(1)
     partial(0, 1)
     partial(0, -1)
-    y_step(0, 5)
-    y_step(0, 6)
     partial(0, 0)
-    x_last(1)
     core_wait(1)
     partial(1, 4)
     y_step(1, 0)
     partial(1, 3)
     partial(1, -3)
     y_step(1, 1)
-    y_last(0)
-    y_step(1, 2)
+    y_step(0, 4)
+    y_step(0, 5)
     partial(1, 2)
     partial(1, -2)
+    y_step(1, 2)
     y_step(1, 3)
-    y_step(1, 4)
+    y_step(0, 6)
     partial(1, 1)
     partial(1, -1)
     partial(1, 0)
+    y_step(1, 4)
     y_step(1, 5)
+    y_last(0)
     y_step(1, 6)
     y_last(1)
     hidden(0)
-    for s in range(1, 5):
-        h_send(0, s)
-        h_wait(0, s)
-    product(0)
+    h_own(0)
+    h_pass(0)
+    product(0, 0)
+    product(0, -2)
     hidden(1)
-    h_send(1, 1)
-    over_cores(0)
-    h_wait(1, 1)
-    h_send(1, 2)
+    h_own(1)
+    over_cores(0, 0)
+    over_cores(0, -2)
+    h_last(0)
+    product(0, 2)
+    product(0, 4)
+    over_cores(0, 2)
+    over_cores(0, 4)
+    h_pass(1)
+    product(1, 0)
+    product(1, -2)
+    over_cores(1, 0)
+    over_cores(1, -2)
     over_x(0)
-    h_wait(1, 2)
-    h_send(1, 3)
-    h_wait(1, 3)
-    h_send(1, 4)
-    h_wait(1, 4)
-    product(1)
-    over_cores(1)
+    h_last(1)
+    product(1, 2)
+    product(1, 4)
+    over_cores(1, 2)
+    over_cores(1, 4)
     over_x(1)
     over_z()
     for copy in sends:
         copy.wait_send()
+    for k in range(CHUNKS):
+        for q in range(NX):
+            left(csend.at[k, q], crecv.at[k, q], c_s.at[k, q], c_r.at[k, q], sibling)
+            if q:
+                left(xsend.at[k, q], xrecv.at[k, q], x_s.at[k, q], x_r.at[k, q], at_x(q))
 
 
 def body(inputs, cotangent, up_weight, down_weight, up_bias):
@@ -315,6 +376,11 @@
     pack, spread = select_matrices()
     vmem, dma = pltpu.VMEM, pltpu.SemaphoreType.DMA
     scratch = [
+        vmem((W, W), BF16),
+        vmem((W, W), BF16),
+        vmem((1, W), F32),
+        vmem(pack.shape, BF16),
+        vmem(spread.shape, BF16),
         vmem((CHUNKS, NX, NC, SLOTS * SLAB, W), BF16),
         vmem((CHUNKS, NY, 2, BLOCK, W), F32),
         vmem((CHUNKS, 2, 7, BLOCK, W), BF16),
@@ -322,23 +388,24 @@
         vmem((CHUNKS, 2, BLOCK, W), BF16),
         vmem((CHUNKS, 2, BLOCK, W), BF16),
         vmem((CHUNKS, NY, BLOCK, W), BF16),
-        vmem((CHUNKS, NX, NC, BLOCK, W), F32),
+        vmem((CHUNKS, NX, BLOCK, W), F32),
         vmem((CHUNKS, NX, BLOCK, W), BF16),
         vmem((CHUNKS, NX, BLOCK, W), BF16),
-        vmem((CHUNKS, NX - 1, BLOCK, W), BF16),
-        vmem((CHUNKS, NX - 1, BLOCK, W), BF16),
+        vmem((CHUNKS, NX, BLOCK, W), BF16),
+        vmem((CHUNKS, NX, BLOCK, W), BF16),
         vmem((CHUNKS, SLOTS, OUT, W), BF16),
         vmem((CHUNKS, SLOTS, OUT, W), BF16),
     ]
     for shape in (
-        (NZ,), (CHUNKS, 4), (CHUNKS, NX), (CHUNKS, 2, 7), (CHUNKS, 2), (CHUNKS, 2, 4),
-        (CHUNKS,), (CHUNKS, NX - 1), (CHUNKS, SLOTS),
+        (NZ,), (3, NZ), (CHUNKS, NX), (CHUNKS, 2, 7), (CHUNKS, 2), (CHUNKS, 8),
+        (CHUNKS, NX), (CHUNKS, NX), (CHUNKS, SLOTS),
     ):
         scratch += [dma(shape), dma(shape)]
+    scratch.append(dma((5,)))
     return pl.pallas_call(
         kernel,
         out_shape=jax.ShapeDtypeStruct((OWN, W), BF16),
-        in_specs=[pl.BlockSpec(memory_space=pltpu.VMEM)] * 6,
+        in_specs=[pl.BlockSpec(memory_space=pltpu.VMEM)] + [pl.BlockSpec(memory_space=pl.ANY)] * 5,
         out_specs=pl.BlockSpec(memory_space=pltpu.VMEM),
         scratch_shapes=scratch,
         compiler_params=pltpu.CompilerParams(

time: 126 us -> 118 us (0.937)
  Pallas kernels: 121 us -> 113 us
    pallas_call x1, Pallas kernels: 121 us -> 113 us  [body(): pl.pallas_call(kernel, out_shape=jax.ShapeDtypeStruct((OWN, W), BF16), in...]
where the time goes in v2:
time: 118 us
  Pallas kernels  113 us (96%)
  local copies, waits for them, and re-layouts  4.1 us (3%)
    pallas_call x1, Pallas kernels, body(): pl.pallas_call(kernel, out_shape=jax.ShapeDtypeStruct((OWN, W), BF16), in...  113 us
    unnamed x11, local copies, waits for them, and re-layouts  4.02 us

profile of v2, /device:TPU:1, one launch (start us, length us, event | category | flops | bytes accessed | tf_op | source)
XLA Modules:
  0.0 117.9 jit_solution(9271812113889950549)
XLA Ops:
  0.0 0.0 copy-start.4
  0.0 0.1 pad.2.clone
  0.1 0.6 copy-done.4
  0.7 0.0 copy-start.3
  0.7 0.8 maximum_maximum_fusion.slab_ref
  1.5 0.0 copy-done.3
  1.5 0.0 copy-start
  1.5 1.0 copy-done
  2.5 0.0 copy-start.1
  2.5 1.0 copy-done.1
  3.4 0.0 copy-start.2
  3.4 0.9 copy-done.2
  4.3 113.0 %mlp_input_grad.1 = bf16[20,384]{1,0:T(8,128)(2,1)S(1)} custom-call(bf16[48,384]{1,0:T(8,128)(2,1)S(1)} %maximum_maximum_fusion.slab_ref, bf16[384,384]{1,0:T(8,128)(2,1)S(1)} %copy-done, bf16[384,384]{1,0:T(8,128)(2,1)S(1)} %copy-done.1, f32[1,384]{1,0:T(1,128)S(1)} %broadcast_in_dim.7.bias_hbm, bf16[160,192]{1,0:T(8,128)(2,1)S(1)} %copy-done.2, ...), custom_call_target="tpu_custom_call" | custom-call | tf_op jit(solution)/shard_map/mlp_input_grad/pallas_call | solution.py:405
  117.3 0.6 copy.9
  (2 shorter events, 0.0 us)
Async XLA Ops:
  0.0 0.7 copy-start.4
  0.7 0.8 copy-start.3
  1.5 1.0 copy-start
  2.5 1.0 copy-start.1
  3.4 0.9 copy-start.2

commit v3 on v2

v3 whole, which is shorter than its diff:
```python
import functools

import jax
import jax.numpy as jnp
from jax import lax
from jax.experimental import pallas as pl
from jax.experimental.pallas import tpu as pltpu
from jax.sharding import PartitionSpec as P

MESH = pl.DeviceIdType.MESH
BF16, F32 = jnp.bfloat16, jnp.float32

NX, NZ, NC, NY = 4, 8, 2, 8
OWN = 20
W = 384
TILE = 16
WIDE = W + 128
SLAB = 2 * TILE
CHUNKS, SLOTS = 2, 4
BLOCK = SLOTS * OWN

OFFSETS = ((0, 1, 7, 2), (6, 3, 5, 4))
WHERE = {off: (k, j) for k, row in enumerate(OFFSETS) for j, off in enumerate(row)}

PARTS = ((0, 0, 48), (0, 48, 32), (1, 0, 48), (1, 48, 32))

SQRT_2_OVER_PI = 0.7978845608028654
CUBE = 0.044715


def grid_of(rows, columns):
    shape = (rows, columns)
    return lax.broadcasted_iota(jnp.int32, shape, 0), lax.broadcasted_iota(jnp.int32, shape, 1)


def ones_where(mask):
    return jnp.where(mask, 1.0, 0.0).astype(BF16)


def tail_select(group, row, column):
    return (row >= 4 * group) & (row < 4 * group + 4) & (column == TILE + row - 4 * group)


def pack_own(ref):
    i, j = grid_of(TILE, OWN)
    tail = jnp.zeros((TILE, 128), F32)
    for g in range(3):
        tail += dot(ones_where(tail_select(g, i, j)), ref[:, 128 * g : 128 * g + 128])
    return ref[0:TILE, :], tail.astype(BF16)


def unpack_select():
    i, s = grid_of(2 * BLOCK, SLOTS * SLAB)
    kind = (i >= BLOCK).astype(jnp.int32)
    r = i - BLOCK * kind
    slot = sum((r >= OWN * j).astype(jnp.int32) for j in range(1, SLOTS))
    r = r - OWN * slot
    at = SLAB * slot + TILE * kind
    yield ones_where((r < TILE) & (s == at + r))
    for g in range(3):
        yield ones_where((r >= TILE) & (s == at + 4 * g + r - TILE))


def spread_select():
    o, i = grid_of(SLOTS * TILE, BLOCK)
    slot = sum((o >= TILE * j).astype(jnp.int32) for j in range(1, SLOTS))
    r, i = o - TILE * slot, i - OWN * slot
    yield ones_where(i == r)
    for g in range(3):
        yield ones_where(tail_select(g, r, i))


def unpack_out(packed):
    r, s = grid_of(OWN, TILE)
    main = dot(ones_where((r < TILE) & (s == r)), packed[:, :W])
    tails = [dot(ones_where((r >= TILE) & (s == 4 * g + r - TILE)), packed[:, W:]) for g in range(3)]
    return main + jnp.concatenate(tails, axis=1)


def dot(a, b):
    return jnp.dot(a, b, preferred_element_type=F32)


def dot_t(a, b):
    return lax.dot_general(a, b, (((1,), (1,)), ((), ())), preferred_element_type=F32)


def gelu_slope(v):
    u = SQRT_2_OVER_PI * (v + CUBE * (v * v * v))
    t = jnp.tanh(u)
    du = SQRT_2_OVER_PI * (1.0 + (3.0 * CUBE) * (v * v))
    return 0.5 * (1.0 + t) + 0.5 * v * (1.0 - t * t) * du


def kernel(
    x_ref, cot_ref, up_hbm, down_hbm, bias_hbm, out_ref,
    up_ref, down_ref, bias_ref, slab_ref, pack_ref, spread_ref,
    gath, part, ysend, yrecv, zsend, zrecv, hid, prod, csend, crecv, xsend, xrecv, fsend, frecv,
    az_s, az_r, ax_s, ax_r, ac_s, ac_r, y_s, y_r, zh_s, zh_r, h_s, h_r, c_s, c_r, x_s, x_r, f_s, f_r, load_s,
):
    d, t = lax.axis_index("dp"), lax.axis_index("tensor")
    x, z, c = d // (NZ * NC), (d // NC) % NZ, d % NC
    y, zh = t // 2, t % 2
    ring = jnp.where(z % 2 == 0, z // 2, NZ - 1 - z // 2)

    def dev(x=x, z=z, c=c, y=y, zh=zh):
        return ((x * NZ + z) * NC + c, y * 2 + zh)

    def at_ring(off):
        r = (ring + off) % NZ
        return dev(z=jnp.where(r < NZ // 2, 2 * r, 2 * NZ - 1 - 2 * r))

    def at_x(off):
        return dev(x=(x + off) % NX)

    def at_y(off):
        return dev(y=(y + off) % NY)

    sibling, far = dev(c=1 - c), dev(zh=1 - zh)

    sends = []

    def send(src, dst, ssem, rsem, device, keep=True):
        copy = pltpu.make_async_remote_copy(
            src_ref=src, dst_ref=dst, send_sem=ssem, recv_sem=rsem, device_id=device, device_id_type=MESH
        )
        copy.start()
        if keep:
            sends.append(copy)

    def arrived(ref, rsem):
        pltpu.make_async_copy(ref, ref, rsem).wait()

    def left(src, dst, ssem, rsem, device):
        pltpu.make_async_remote_copy(
            src_ref=src, dst_ref=dst, send_sem=ssem, recv_sem=rsem, device_id=device, device_id_type=MESH
        ).wait_send()

    loads = []
    for i, (src, dst) in enumerate(
        ((up_hbm, up_ref), (down_hbm, down_ref), (bias_hbm, bias_ref))
    ):
        loads.append(pltpu.make_async_copy(src, dst, load_s.at[i]))
        loads[-1].start()

    peers = [sibling, far, at_y(1), at_y(-1)]
    peers += [at_x(o) for o in range(1, NX)] + [at_ring(o) for o in range(1, NZ)]
    barrier = pltpu.get_barrier_semaphore()
    for peer in peers:
        pl.semaphore_signal(barrier, inc=1, device_id=peer, device_id_type=MESH)
    for i, ref in enumerate((x_ref, cot_ref)):
        rows = slice(TILE * i, TILE * i + TILE)
        slab_ref[rows, :W], slab_ref[rows, W:] = pack_own(ref)
    gath[0, 0, pl.ds(c, 1), 0:SLAB, :] = slab_ref[...][None]
    pl.semaphore_wait(barrier, len(peers))

    def slot(off, q=0, rows=SLAB, start=0):
        k, j = WHERE[off % NZ]
        return gath.at[k, q % NX, c, pl.ds(SLAB * j + start, rows)]

    def z_own():
        for way in (2, -2, 1, -1):
            at = -way % NZ
            send(slab_ref, slot(at), az_s.at[at], az_r.at[at], at_ring(way))
        x_send(0)

    def z_pass(way):
        off = -2 * way % NZ
        arrived(slot(off), az_r.at[off])
        at = -3 * way % NZ
        send(slot(off), slot(at), az_s.at[at], az_r.at[at], at_ring(way))
        rows, start, i = (TILE, 0, 4) if way == 1 else (TILE, TILE, 0)
        send(slot(off, 0, rows, start), slot(4, 0, rows, start), az_s.at[i], az_r.at[i], at_ring(2 * way))
        x_send(off)

    def z_take(off):
        off %= NZ
        if off == 4:
            arrived(slot(4, 0, TILE, 0), az_r.at[4])
            arrived(slot(4, 0, TILE, TILE), az_r.at[0])
        else:
            arrived(slot(off), az_r.at[off])
        x_send(off)

    def x_send(off):
        for i, way in enumerate((1, -1)):
            src = slab_ref if off == 0 else slot(off)
            send(src, slot(off, -way), ax_s.at[i, off], ax_r.at[i, off], at_x(way))

    def x_take(off):
        off %= NZ
        for i, way in enumerate((1, -1)):
            arrived(slot(off, -way), ax_r.at[i, off])
            if i == WHERE[off][1] % 2:
                send(slot(off, -way), slot(off, 2), ax_s.at[2, off], ax_r.at[2, off], at_x(way))

    def x_last(k):
        for off in OFFSETS[k]:
            arrived(slot(off, 2), ax_r.at[2, off])
        core_send(k, 2)

    def core_send(k, q):
        send(gath.at[k, q, c], gath.at[k, q, c], ac_s.at[k, q], ac_r.at[k, q], sibling)

    def core_wait(k):
        for q in range(NX):
            arrived(gath.at[k, q, 1 - c], ac_r.at[k, q])

    def selects():
        for i, m in enumerate(unpack_select()):
            pack_ref[i] = m
        for i, m in enumerate(spread_select()):
            spread_ref[i] = m

    def partial(k, dist):
        o = (y + dist) % NY
        slabs = gath[k, o // NC, o % NC]
        tails = [dot(pack_ref[1 + g], slabs[:, W:]) for g in range(3)]
        rows = (dot(pack_ref[0], slabs[:, :W]) + jnp.concatenate(tails, axis=1)).astype(BF16)
        part[k, dist % NY, 0] = dot(rows[:BLOCK], up_ref[...])
        part[k, dist % NY, 1] = dot_t(rows[BLOCK:], down_ref[...])

    def rows_of(p):
        k, start, rows = PARTS[p]
        return k, pl.ds(start, rows)

    def y_step(p, m):
        k, rows = rows_of(p)
        dist = 4 - (m + 1) // 2
        for i, way in enumerate((1, -1)):
            which = (m + 1 + i) % 2
            total = part[k, (way * dist) % NY, which, rows, :]
            if m >= 2:
                arrived(yrecv.at[k, i, m - 2, rows], y_r.at[p, i, m - 2])
                total = total + yrecv[k, i, m - 2, rows, :].astype(F32)
            ysend[k, i, m, rows, :] = total.astype(BF16)
            send(ysend.at[k, i, m, rows], yrecv.at[k, i, m, rows], y_s.at[p, i, m], y_r.at[p, i, m], at_y(way))

    def y_last(p):
        k, rows = rows_of(p)
        for which in range(2):
            total = part[k, 0, which, rows, :]
            for i, m in ((0, 5 + which), (1, 6 - which)):
                arrived(yrecv.at[k, i, m, rows], y_r.at[p, i, m])
                total = total + yrecv[k, i, m, rows, :].astype(F32)
            part[k, 0, which, rows, :] = total
            zsend[k, which, rows, :] = total.astype(BF16)
            send(zsend.at[k, which, rows], zrecv.at[k, which, rows], zh_s.at[p, which], zh_r.at[p, which], far)

    def hidden(p):
        k, rows = rows_of(p)
        arrived(zrecv.at[k, 0, rows], zh_r.at[p, 0])
        slope = gelu_slope(part[k, 0, 0, rows, :] + zrecv[k, 0, rows, :].astype(F32) + bias_ref[...])
        arrived(zrecv.at[k, 1, rows], zh_r.at[p, 1])
        value = ((part[k, 0, 1, rows, :] + zrecv[k, 1, rows, :].astype(F32)) * slope).astype(BF16)
        hid[k, pl.ds(y, 1), rows, :] = value[None]

    def h_block(p, dist, side=None):
        k, start, rows = PARTS[p]
        if side is not None:
            first = 32 if rows == 48 else 16
            start, rows = (start, first) if side == 0 else (start + first, rows - first)
        return hid.at[k, (y + dist + NY) % NY, pl.ds(start, rows)]

    def h_copy(p, dist, way, i, side=None):
        piece = h_block(p, dist, side)
        send(piece, piece, h_s.at[p, i], h_r.at[p, i], at_y(way))

    def h_own(p):
        for i, way in enumerate((2, -2, 1, -1)):
            h_copy(p, 0, way, i)

    def h_pass(p):
        for i, way in enumerate((1, -1)):
            arrived(h_block(p, -2 * way), h_r.at[p, i])
            h_copy(p, -2 * way, way, 4 + i)
            h_copy(p, -2 * way, 2 * way, 6 + i, i)

    def h_near(p):
        for i, way in enumerate((1, -1)):
            arrived(h_block(p, -way), h_r.at[p, 2 + i])

    def h_last(p):
        for i, way in enumerate((1, -1)):
            arrived(h_block(p, -3 * way), h_r.at[p, 4 + i])
            arrived(h_block(p, 4, i), h_r.at[p, 6 + i])

    def pair(dist, own):
        first = y + dist + NY
        o = (first + (first + c + (0 if own else 1)) % 2) % NY
        return o // NC, o

    def product(k, dist):
        q, o = pair(dist, False)
        csend[k, q] = dot_t(hid[k, o], up_ref[...]).astype(BF16)
        send(csend.at[k, q], crecv.at[k, q], c_s.at[k, q], c_r.at[k, q], sibling, False)
        q, o = pair(dist, True)
        prod[k, q] = dot_t(hid[k, o], up_ref[...])

    def over_cores(k, dist):
        q, _ = pair(dist, True)
        arrived(crecv.at[k, q], c_r.at[k, q])
        total = prod[k, q] + crecv[k, q].astype(F32)
        prod[k, q] = total
        xsend[k, q] = total.astype(BF16)

        @pl.when(q != 0)
        def _():
            send(xsend.at[k, q], xrecv.at[k, q], x_s.at[k, q], x_r.at[k, q], at_x(q), False)

    def over_x(k):
        total = prod[k, 0]
        for q in (1, 3, 2):
            arrived(xrecv.at[k, q], x_r.at[k, q])
            total = total + xrecv[k, q].astype(F32)
        total = total.astype(BF16)
        fsend[k, :, :W] = dot(spread_ref[0], total).astype(BF16)
        tails = [dot(spread_ref[1 + g], total[:, 128 * g : 128 * g + 128]) for g in range(3)]
        fsend[k, :, W:] = (tails[0] + tails[1] + tails[2]).astype(BF16)
        for j in range(SLOTS):
            off, rows = OFFSETS[k][j], pl.ds(TILE * j, TILE)
            if off:
                send(fsend.at[k, rows], frecv.at[k, rows], f_s.at[k, j], f_r.at[k, j], at_ring(off))

    def over_z():
        total = fsend[0, 0:TILE, :].astype(F32)
        for k in range(CHUNKS):
            for j in range(SLOTS):
                rows = pl.ds(TILE * j, TILE)
                if OFFSETS[k][j]:
                    arrived(frecv.at[k, rows], f_r.at[k, j])
                    total = total + frecv[k, rows, :].astype(F32)
        out_ref[...] = unpack_out(total.astype(BF16)).astype(BF16)

    z_own()
    selects()
    x_take(0)
    z_pass(1)
    z_pass(-1)
    z_take(1)
    z_take(-1)
    core_send(0, 0)
    x_take(2)
    x_take(-2)
    x_take(1)
    x_take(-1)
    core_send(0, 1)
    core_send(0, 3)
    z_take(3)
    z_take(-3)
    z_take(4)
    core_send(1, 0)
    x_last(0)
    for load in loads:
        load.wait()
    core_wait(0)
    partial(0, 4)
    y_step(0, 0)
    y_step(1, 0)
    partial(0, 3)
    partial(0, -3)
    y_step(0, 1)
    y_step(1, 1)
    x_take(3)
    x_take(-3)
    x_take(4)
    core_send(1, 1)
    core_send(1, 3)
    partial(0, 2)
    partial(0, -2)
    y_step(0, 2)
    y_step(0, 3)
    y_step(1, 2)
    y_step(1, 3)
    x_last(1)
    partial(0, 1)
    partial(0, -1)
    partial(0, 0)
    core_wait(1)
    partial(1, 4)
    y_step(2, 0)
    y_step(3, 0)
    partial(1, 3)
    partial(1, -3)
    y_step(2, 1)
    y_step(0, 4)
    y_step(0, 5)
    y_step(1, 4)
    y_step(1, 5)
    y_step(3, 1)
    partial(1, 2)
    partial(1, -2)
    y_step(0, 6)
    y_last(0)
    y_step(2, 2)
    y_step(2, 3)
    y_step(1, 6)
    y_last(1)
    y_step(3, 2)
    y_step(3, 3)
    partial(1, 1)
    partial(1, -1)
    partial(1, 0)
    y_step(2, 4)
    y_step(2, 5)
    y_step(3, 4)
    y_step(3, 5)
    y_step(2, 6)
    y_last(2)
    y_step(3, 6)
    y_last(3)
    hidden(0)
    h_own(0)
    hidden(1)
    h_own(1)
    h_pass(0)
    h_pass(1)
    h_near(0)
    h_near(1)
    product(0, 0)
    product(0, -2)
    hidden(2)
    h_own(2)
    over_cores(0, 0)
    over_cores(0, -2)
    h_last(0)
    h_last(1)
    product(0, 2)
    hidden(3)
    h_own(3)
    product(0, 4)
    over_cores(0, 2)
    over_cores(0, 4)
    h_pass(2)
    h_pass(3)
    over_x(0)
    h_near(2)
    h_near(3)
    product(1, 0)
    product(1, -2)
    over_cores(1, 0)
    over_cores(1, -2)
    h_last(2)
    h_last(3)
    product(1, 2)
    product(1, 4)
    over_cores(1, 2)
    over_cores(1, 4)
    over_x(1)
    over_z()
    for copy in sends:
        copy.wait_send()
    for k in range(CHUNKS):
        for q in range(NX):
            left(csend.at[k, q], crecv.at[k, q], c_s.at[k, q], c_r.at[k, q], sibling)
            if q:
                left(xsend.at[k, q], xrecv.at[k, q], x_s.at[k, q], x_r.at[k, q], at_x(q))


def body(inputs, cotangent, up_weight, down_weight, up_bias):
    vmem, dma = pltpu.VMEM, pltpu.SemaphoreType.DMA
    scratch = [
        vmem((W, W), BF16),
        vmem((W, W), BF16),
        vmem((1, W), F32),
        vmem((SLAB, WIDE), BF16),
        vmem((4, 2 * BLOCK, SLOTS * SLAB), BF16),
        vmem((4, SLOTS * TILE, BLOCK), BF16),
        vmem((CHUNKS, NX, NC, SLOTS * SLAB, WIDE), BF16),
        vmem((CHUNKS, NY, 2, BLOCK, W), F32),
        vmem((CHUNKS, 2, 7, BLOCK, W), BF16),
        vmem((CHUNKS, 2, 7, BLOCK, W), BF16),
        vmem((CHUNKS, 2, BLOCK, W), BF16),
        vmem((CHUNKS, 2, BLOCK, W), BF16),
        vmem((CHUNKS, NY, BLOCK, W), BF16),
        vmem((CHUNKS, NX, BLOCK, W), F32),
        vmem((CHUNKS, NX, BLOCK, W), BF16),
        vmem((CHUNKS, NX, BLOCK, W), BF16),
        vmem((CHUNKS, NX, BLOCK, W), BF16),
        vmem((CHUNKS, NX, BLOCK, W), BF16),
        vmem((CHUNKS, SLOTS * TILE, WIDE), BF16),
        vmem((CHUNKS, SLOTS * TILE, WIDE), BF16),
    ]
    for shape in (
        (NZ,), (3, NZ), (CHUNKS, NX), (len(PARTS), 2, 7), (len(PARTS), 2), (len(PARTS), 8),
        (CHUNKS, NX), (CHUNKS, NX), (CHUNKS, SLOTS),
    ):
        scratch += [dma(shape), dma(shape)]
    scratch.append(dma((3,)))
    return pl.pallas_call(
        kernel,
        out_shape=jax.ShapeDtypeStruct((OWN, W), BF16),
        in_specs=[pl.BlockSpec(memory_space=pltpu.VMEM)] * 2 + [pl.BlockSpec(memory_space=pl.ANY)] * 3,
        out_specs=pl.BlockSpec(memory_space=pltpu.VMEM),
        scratch_shapes=scratch,
        compiler_params=pltpu.CompilerParams(
            collective_id=0, has_side_effects=True, vmem_limit_bytes=60 << 20
        ),
        name="mlp_input_grad",
    )(inputs, cotangent, up_weight, down_weight, up_bias[None, :])


def solution(mesh):
    return jax.shard_map(
        body,
        mesh=mesh,
        in_specs=(
            P("dp", "tensor"),
            P("dp", "tensor"),
            P("tensor", "dp"),
            P("dp", "tensor"),
            P("dp"),
        ),
        out_specs=P("dp", "tensor"),
        check_vma=False,
    )
```

time: 118 us -> 111 us (0.941)
  Pallas kernels: 113 us -> 108 us
  local copies, waits for them, and re-layouts: 4.1 us -> 2.57 us
    pallas_call x1, Pallas kernels: 113 us -> 108 us  [body(): pl.pallas_call(kernel, out_shape=jax.ShapeDtypeStruct((OWN, W), BF16), in...]
    unnamed x11 -> x1, local copies, waits for them, and re-layouts: 4.02 us -> 1.33 us
    broadcast_in_dim x1, local copies, waits for them, and re-layouts: 0.01 us -> 1.24 us  [body(): up_bias[None, :]]
where the time goes in v3:
time: 111 us
  Pallas kernels  108 us (97%)
  local copies, waits for them, and re-layouts  2.57 us (2%)
    pallas_call x1, Pallas kernels, body(): pl.pallas_call(kernel, out_shape=jax.ShapeDtypeStruct((OWN, W), BF16), in...  108 us

profile of v3, /device:TPU:1, one launch (start us, length us, event | category | flops | bytes accessed | tf_op | source)
XLA Modules:
  0.0 110.8 jit_solution(3235828370325252186)
XLA Ops:
  0.0 1.2 %broadcast_in_dim.3.bias_hbm = f32[1,384]{1,0:T(1,128)} reshape(f32[384]{0:T(512)} %param.9) | data formatting | bytes 3072 | tf_op jit(solution)/shard_map/broadcast_in_dim | solution.py:500
  1.2 108.2 %mlp_input_grad.1 = bf16[20,384]{1,0:T(8,128)(2,1)} custom-call(bf16[20,384]{1,0:T(8,128)(2,1)} %x_ref.1, bf16[20,384]{1,0:T(8,128)(2,1)} %cot_ref.1, bf16[384,384]{1,0:T(8,128)(2,1)} %up_hbm.1, bf16[384,384]{1,0:T(8,128)(2,1)} %down_hbm.1, f32[1,384]{1,0:T(1,128)} %broadcast_in_dim.3.bias_hbm), custom_call_target="tpu_custom_call" | custom-call | tf_op jit(solution)/shard_map/mlp_input_grad/pallas_call | solution.py:490
  109.5 1.3 %copy.7 = bf16[20,384]{1,0:T(8,128)(2,1)} copy(bf16[20,384]{1,0:T(8,128)(2,1)} %mlp_input_grad.1) | data formatting | bytes 30720

commit v4 on v3

--- a/solution.py
+++ b/solution.py
@@ -250,7 +250,7 @@
     def hidden(p):
         k, rows = rows_of(p)
         arrived(zrecv.at[k, 0, rows], zh_r.at[p, 0])
-        slope = gelu_slope(part[k, 0, 0, rows, :] + zrecv[k, 0, rows, :].astype(F32) + bias_ref[...])
+        slope = gelu_slope(part[k, 0, 0, rows, :] + zrecv[k, 0, rows, :].astype(F32) + bias_ref[...][None, :])
         arrived(zrecv.at[k, 1, rows], zh_r.at[p, 1])
         value = ((part[k, 0, 1, rows, :] + zrecv[k, 1, rows, :].astype(F32)) * slope).astype(BF16)
         hid[k, pl.ds(y, 1), rows, :] = value[None]
@@ -354,93 +354,93 @@
     for load in loads:
         load.wait()
     core_wait(0)
+    x_take(-3)
+    x_take(3)
+    x_take(4)
+    core_send(1, 1)
+    core_send(1, 3)
     partial(0, 4)
     y_step(0, 0)
-    y_step(1, 0)
     partial(0, 3)
     partial(0, -3)
     y_step(0, 1)
+    partial(0, 2)
+    y_step(1, 0)
     y_step(1, 1)
-    x_take(3)
-    x_take(-3)
-    x_take(4)
-    core_send(1, 1)
-    core_send(1, 3)
-    partial(0, 2)
     partial(0, -2)
     y_step(0, 2)
+    partial(0, 0)
+    partial(0, 1)
     y_step(0, 3)
+    partial(0, -1)
     y_step(1, 2)
     y_step(1, 3)
     x_last(1)
-    partial(0, 1)
-    partial(0, -1)
-    partial(0, 0)
+    y_step(0, 4)
     core_wait(1)
+    y_step(0, 5)
+    partial(1, -3)
+    y_step(1, 4)
+    y_step(1, 5)
+    partial(1, 3)
+    y_step(0, 6)
     partial(1, 4)
     y_step(2, 0)
+    y_step(2, 1)
+    partial(1, -2)
+    y_step(1, 6)
+    partial(1, 2)
     y_step(3, 0)
-    partial(1, 3)
-    partial(1, -3)
-    y_step(2, 1)
-    y_step(0, 4)
-    y_step(0, 5)
-    y_step(1, 4)
-    y_step(1, 5)
     y_step(3, 1)
-    partial(1, 2)
-    partial(1, -2)
-    y_step(0, 6)
     y_last(0)
+    partial(1, 0)
     y_step(2, 2)
+    partial(1, -1)
     y_step(2, 3)
-    y_step(1, 6)
+    partial(1, 1)
+    y_step(3, 2)
     y_last(1)
-    y_step(3, 2)
     y_step(3, 3)
-    partial(1, 1)
-    partial(1, -1)
-    partial(1, 0)
     y_step(2, 4)
     y_step(2, 5)
     y_step(3, 4)
     y_step(3, 5)
     y_step(2, 6)
+    y_step(3, 6)
     y_last(2)
-    y_step(3, 6)
-    y_last(3)
     hidden(0)
     h_own(0)
+    y_last(3)
     hidden(1)
     h_own(1)
     h_pass(0)
+    h_near(0)
     h_pass(1)
-    h_near(0)
     h_near(1)
     product(0, 0)
     product(0, -2)
+    h_last(0)
     hidden(2)
     h_own(2)
+    over_cores(0, -2)
     over_cores(0, 0)
-    over_cores(0, -2)
-    h_last(0)
     h_last(1)
     product(0, 2)
+    product(0, 4)
+    over_cores(0, 2)
     hidden(3)
     h_own(3)
-    product(0, 4)
-    over_cores(0, 2)
+    h_pass(2)
     over_cores(0, 4)
-    h_pass(2)
+    h_near(2)
     h_pass(3)
+    h_near(3)
+    product(1, -2)
+    product(1, 0)
     over_x(0)
-    h_near(2)
-    h_near(3)
-    product(1, 0)
-    product(1, -2)
-    over_cores(1, 0)
     over_cores(1, -2)
     h_last(2)
+    over_cores(1, 0)
     h_last(3)
     product(1, 2)
     product(1, 4)
@@ -462,7 +462,7 @@
     scratch = [
         vmem((W, W), BF16),
         vmem((W, W), BF16),
-        vmem((1, W), F32),
+        vmem((W,), F32),
         vmem((SLAB, WIDE), BF16),
         vmem((4, 2 * BLOCK, SLOTS * SLAB), BF16),
         vmem((4, SLOTS * TILE, BLOCK), BF16),
@@ -497,7 +497,7 @@
             collective_id=0, has_side_effects=True, vmem_limit_bytes=60 << 20
         ),
         name="mlp_input_grad",
-    )(inputs, cotangent, up_weight, down_weight, up_bias[None, :])
+    )(inputs, cotangent, up_weight, down_weight, up_bias)
 
 
 def solution(mesh):

time: 111 us -> 108 us (0.973)
  Pallas kernels: 108 us -> 106 us
  local copies, waits for them, and re-layouts: 2.57 us -> 1.33 us
    pallas_call x1, Pallas kernels: 108 us -> 106 us  [body(): pl.pallas_call(kernel, out_shape=jax.ShapeDtypeStruct((OWN, W), BF16), in...]
    broadcast_in_dim x1 -> x0, local copies, waits for them, and re-layouts: 1.24 us -> none  [body(): up_bias[None, :]]
where the time goes in v4:
time: 108 us
  Pallas kernels  106 us (98%)
  local copies, waits for them, and re-layouts  1.33 us (1%)
    pallas_call x1, Pallas kernels, body(): pl.pallas_call(kernel, out_shape=jax.ShapeDtypeStruct((OWN, W), BF16), in...  106 us

profile of v4, /device:TPU:1, one launch (start us, length us, event | category | flops | bytes accessed | tf_op | source)
XLA Modules:
  0.0 107.6 jit_solution(5360048633107443681)
XLA Ops:
  0.0 106.2 %mlp_input_grad.1 = bf16[20,384]{1,0:T(8,128)(2,1)} custom-call(bf16[20,384]{1,0:T(8,128)(2,1)} %x_ref.1, bf16[20,384]{1,0:T(8,128)(2,1)} %cot_ref.1, bf16[384,384]{1,0:T(8,128)(2,1)} %up_hbm.1, bf16[384,384]{1,0:T(8,128)(2,1)} %down_hbm.1, f32[384]{0:T(512)} %bias_hbm.1), custom_call_target="tpu_custom_call" | custom-call | tf_op jit(solution)/shard_map/mlp_input_grad/pallas_call | solution.py:490
  106.2 1.3 %copy.7 = bf16[20,384]{1,0:T(8,128)(2,1)} copy(bf16[20,384]{1,0:T(8,128)(2,1)} %mlp_input_grad.1) | data formatting | bytes 30720
